TPU v7x, 256 devices: a whole 4x4x8 slice. The times are simulated.
256 devices in a mesh: dp: 8 (over y, core), space: 32 (over z, x).
Axes of the slice: x: 4, y: 4, z: 8, core: 2. Of those that a mesh axis runs over, the one named last changes fastest.
Arguments:
- features: bfloat16 [8, 32, 512, 256], P('dp', 'space'), may hold values from -6 to 6
- occupancy: int32 [8, 32, 512], P('dp', 'space'), may hold values 0 or 1
- nbr_slots: int32 [8, 32, 26], P('dp', 'space'), may hold values from 0 to 6, as said below
- send_mask: int32 [8, 32, 6], P('dp', 'space'), may hold values from 0 to 1, as said below
- cotangent: bfloat16 [8, 32, 512, 256], P('dp', 'space'), may hold values from -0.06591797 to 0.06591797
- weight_one: bfloat16 [27, 256, 256], replicated, may hold values from -0.078125 to 0.078125
- weight_two: bfloat16 [27, 256, 256], replicated, may hold values from -0.078125 to 0.078125
Outputs:
- grad_one: float32 [256, 27, 256], P('space')
- grad_two: float32 [256, 27, 256], P('space')
Inputs may be any that keep to these rules, and one draw needn't show every extreme that they name: Bricks of a scene lie in curve order: every brick adjacent to brick i (the 26 brick offsets) is brick i + d with 1 <= |d| <= 3, and nbr_slots names exactly these, 6 elsewhere. send_mask[i, s] is 1 exactly where brick i + d_s has brick i among its neighbours.
All inputs are finite; a program needn't handle non-finite values. No bound on the sum of `occupancy` on one device may be relied on, other than what follows from the above.
Results may differ from a plain program's by a relative error of at most 0.0042.
Values may be sent and summed in bfloat16 or wider, within the bound.
A program may use at most 128 MiB of HBM per device.

v0:
```python
import jax
import jax.numpy as jnp
from jax import lax
from jax.sharding import PartitionSpec as P

E = 8


OFFSETS = [(a, b, c) for a in (-1, 0, 1) for b in (-1, 0, 1) for c in (-1, 0, 1)]
DISTANCES = (-3, -2, -1, 1, 2, 3)


def passed_along(block, axis, distance):
    devices = range(lax.axis_size(axis))
    route = [(i - distance, i) for i in devices if i - distance in devices]
    return lax.ppermute(block, axis, route)


def pick_range(shift, brick_edge):
    if shift == -1:
        return slice(brick_edge - 1, brick_edge)
    if shift == 0:
        return slice(0, brick_edge)
    return slice(0, 1)


def assemble(own_brick, table, slot_row, brick_edge):
    planes = []
    for a in (-1, 0, 1):
        rows_out = []
        for b in (-1, 0, 1):
            pieces = []
            for c in (-1, 0, 1):
                number = (a + 1) * 9 + (b + 1) * 3 + (c + 1)
                if number == 13:
                    block = own_brick
                else:
                    index = number if number < 13 else number - 1
                    block = lax.dynamic_index_in_dim(table, slot_row[index], 0, keepdims=False)
                pieces.append(
                    block[
                        pick_range(a, brick_edge),
                        pick_range(b, brick_edge),
                        pick_range(c, brick_edge),
                    ]
                )
            rows_out.append(jnp.concatenate(pieces, axis=2))
        planes.append(jnp.concatenate(rows_out, axis=1))
    return jnp.concatenate(planes, axis=0)


def windows(padded, brick_edge):
    chans = padded.shape[-1]
    return jnp.stack(
        [
            padded[
                1 + a : 1 + a + brick_edge, 1 + b : 1 + b + brick_edge, 1 + c : 1 + c + brick_edge
            ].reshape(brick_edge**3, chans)
            for a, b, c in OFFSETS
        ]
    )


def silu_slope(value):
    sig = jax.nn.sigmoid(value)
    return sig * (1.0 + value * (1.0 - sig))


def reduce_grads(wins, grad):
    mine = lax.psum_scatter(
        jnp.einsum("kvc,vd->ckd", wins, grad, preferred_element_type=jnp.float32),
        "space",
        scatter_dimension=0,
        tiled=True,
    )
    return lax.psum(mine, "dp")


def local(features, occupancy, nbr_slots, send_mask, cotangent, weight_one, weight_two):
    voxels = features.shape[2]
    chans = features.shape[3]
    own_brick = features[0, 0]
    occupied = occupancy[0, 0].astype(jnp.float32)[:, None]
    slot_row = nbr_slots[0, 0]
    send_flags = send_mask[0, 0].astype(jnp.bfloat16)

    def gather_halo(field):
        received = []
        for position in range(6):
            sent = field * send_flags[5 - position]
            arrived = passed_along(sent, "space", -DISTANCES[position])
            received.append(arrived)
        received.append(jnp.zeros((voxels, chans), jnp.bfloat16))
        table = jnp.stack(received).reshape(7, E, E, E, chans)
        return assemble(field.reshape(E, E, E, chans), table, slot_row, E)

    masked = own_brick * occupancy[0, 0].astype(jnp.bfloat16)[:, None]
    in_windows = windows(gather_halo(masked), E)
    pre_one = (
        jnp.einsum("kvc,kcd->vd", in_windows, weight_one, preferred_element_type=jnp.float32)
        * occupied
    )
    hidden = (pre_one * jax.nn.sigmoid(pre_one)).astype(jnp.bfloat16)
    hidden_windows = windows(gather_halo(hidden), E)
    pre_two = jnp.einsum(
        "kvc,kcd->vd", hidden_windows, weight_two, preferred_element_type=jnp.float32
    ) * occupied + masked.astype(jnp.float32)
    grad_out = (cotangent[0, 0].astype(jnp.float32) * silu_slope(pre_two) * occupied).astype(
        jnp.bfloat16
    )
    grad_windows = windows(gather_halo(grad_out), E)
    grad_two = reduce_grads(hidden_windows, grad_out)
    grad_hidden = jnp.einsum(
        "kvd,kcd->vc", grad_windows[::-1], weight_two, preferred_element_type=jnp.float32
    )
    grad_pre = (grad_hidden * silu_slope(pre_one) * occupied).astype(jnp.bfloat16)
    grad_one = reduce_grads(in_windows, grad_pre)
    return (grad_one, grad_two)


def solution(mesh):
    in_specs = (
        P("dp", "space", None, None),
        P("dp", "space", None),
        P("dp", "space", None),
        P("dp", "space", None),
        P("dp", "space", None, None),
        P(),
        P(),
    )
    out_specs = (P("space", None, None), P("space", None, None))
    return jax.shard_map(local, mesh=mesh, in_specs=in_specs, out_specs=out_specs, check_vma=False)
```

profile of v0, /device:TPU:1, one launch (start us, length us, event | category | flops | bytes accessed | tf_op | source)
XLA Modules:
  0.0 728.1 jit_solution(653469246345885167)
XLA Ops:
  9.4 6.0 broadcast_multiply_fusion.3
  15.5 5.9 collective-permute-start
  21.4 4.5 collective-permute-start.1
  25.9 2.5 collective-permute-start.2
  31.7 1.8 broadcast_multiply_fusion
  90.1 5.5 collective-permute-done.5
  102.1 3.9 copy-done.8
  106.0 3.5 broadcast_multiply_fusion.2
  109.5 3.2 broadcast_multiply_fusion.5
  112.7 4.0 collective-permute-start.6
  116.7 3.7 collective-permute-start.7
  120.4 3.1 collective-permute-start.8
  127.6 1.7 collective-permute-done.8
  129.3 2.5 collective-permute-done.9
  131.8 5.4 collective-permute-done.10
  137.3 4.1 collective-permute-done.11
  147.8 7.3 broadcast_multiply_fusion.1
  155.7 5.0 convolution_bitcast_fusion
  160.7 10.3 %copy.16 = f32[256,27,256]{2,1,0:T(8,128)} copy(f32[256,27,256]{0,2,1:T(8,128)} %convolution_bitcast_fusion) | data formatting | bytes 14155776 | tf_op jit(solution)/shard_map/kvc,vd->ckd/transpose | solution.py:71
  171.1 2.2 collective-permute-start.12
  173.3 10.1 %collective-permute-start.13 = (bf16[512,256]{1,0:T(8,128)(2,1)}, bf16[512,256]{1,0:T(8,128)(2,1)S(1)}, u32[]{:S(2)}, u32[]{:S(2)}) collective-permute-start(bf16[512,256]{1,0:T(8,128)(2,1)} %get-tuple-element.178), channel_id=1, source_target_pairs={{0,2},{1,3},{2,4},{3,5},{4,6},{5,7},{6,8},{7,9},{8,10},{9,11},{10,... | collective-permute-start | bytes 786440 | tf_op jit(solution)/shard_map/ppermute | solution.py:16
  187.3 1.5 collective-permute-start.17
  189.9 6.6 collective-permute-done.15
  196.5 9.7 %collective-permute-done.16 = bf16[512,256]{1,0:T(8,128)(2,1)S(1)} collective-permute-done((bf16[512,256]{1,0:T(8,128)(2,1)}, bf16[512,256]{1,0:T(8,128)(2,1)S(1)}, u32[]{:S(2)}, u32[]{:S(2)}) %collective-permute-start.16) | collective-permute-done | bytes 262176 | tf_op jit(solution)/shard_map/ppermute | solution.py:16
  231.2 6.7 rev.3
  237.9 15.9 %convolution_bitcast_fusion.1 = f32[256,27,256]{0,2,1:T(8,128)} fusion(bf16[27,512,256]{2,1,0:T(8,128)(2,1)} %copy-done.3, bf16[27,512,256]{2,1,0:T(8,128)(2,1)} %rev.3, bf16[27,256,256]{2,1,0:T(8,128)(2,1)S(1)} %copy-done, f32[512,256]{1,0:T(8,128)} %get-tuple-element.221, f32[512]{0:T(512)S(1)} %bitcast.460), kind=kOutput, calls=%fused_computation.1 | convolution fusion | flops 3625189376 | bytes 25298944 | tf_op jit(solution)/shard_map/kvc,vd->ckd/dot_general | solution.py:71
  253.8 10.3 %copy.14 = f32[256,27,256]{2,1,0:T(8,128)} copy(f32[256,27,256]{0,2,1:T(8,128)} %convolution_bitcast_fusion.1) | data formatting | bytes 14155776 | tf_op jit(solution)/shard_map/kvc,vd->ckd/transpose | solution.py:71
  264.2 153.0 %reduce-scatter.5.cloned.1.call-done = f32[8,27,256]{2,1,0:T(8,128)} async-done(((f32[256,27,256]{2,1,0:T(8,128)}), f32[8,27,256]{2,1,0:T(8,128)}) %reduce-scatter.5.cloned.1.call-update) | async-done | bytes 221200 | tf_op jit(solution)/shard_map/reduce_scatter | solution.py:70
  417.2 232.0 %reduce-scatter.3.cloned.1.call-done = f32[8,27,256]{2,1,0:T(8,128)} async-done(((f32[256,27,256]{2,1,0:T(8,128)}), f32[8,27,256]{2,1,0:T(8,128)}) %reduce-scatter.3.cloned.1.call-update) | async-done | bytes 221200 | tf_op jit(solution)/shard_map/reduce_scatter | solution.py:70
  649.3 68.8 %all-reduce.3.cloned.1.call-done = (f32[8,27,256]{2,1,0:T(8,128)}, f32[8,27,256]{2,1,0:T(8,128)}) async-done(((f32[8,27,256]{2,1,0:T(8,128)}, f32[8,27,256]{2,1,0:T(8,128)}), (f32[8,27,256]{2,1,0:T(8,128)}, f32[8,27,256]{2,1,0:T(8,128)})) %all-reduce.3.cloned.1.call-update) | async-done | bytes 442384 | tf_op jit(solution)/shard_map/psum | solution.py:76
  718.0 1.8 copy.17
  719.8 1.8 copy.18
  (258 shorter events, 59.5 us)
Async XLA Ops:
  7.2 139.8 %copy-start = (bf16[27,256,256]{2,1,0:T(8,128)(2,1)S(1)}, bf16[27,256,256]{2,1,0:T(8,128)(2,1)}, u32[]{:S(2)}) copy-start(bf16[27,256,256]{2,1,0:T(8,128)(2,1)} %param.13) | copy-start | bytes 10616836
  7.2 60.4 %copy-start.7 = (s32[1,1,512]{2,1,0:T(1,128)S(1)}, s32[1,1,512]{2,1,0:T(1,128)}, u32[]{:S(2)}) copy-start(s32[1,1,512]{2,1,0:T(1,128)} %param.8) | copy-start | bytes 6148
  7.2 26.3 %copy-start.6 = (s32[1,1,26]{2,1,0:T(1,128)S(1)}, s32[1,1,26]{2,1,0:T(1,128)}, u32[]{:S(2)}) copy-start(s32[1,1,26]{2,1,0:T(1,128)} %param.9) | copy-start | bytes 316
  7.2 410.0 %reduce-scatter.5.cloned.1.call-start = ((), (), s32[]{:S(2)}) async-start(), calls=%async_computation.3 | async-start | bytes 8650752 | tf_op jit(solution)/shard_map/reduce_scatter | solution.py:70
  15.5 68.4 %collective-permute-start = (bf16[512,256]{1,0:T(8,128)(2,1)}, bf16[512,256]{1,0:T(8,128)(2,1)}, u32[]{:S(2)}, u32[]{:S(2)}) collective-permute-start(bf16[512,256]{1,0:T(8,128)(2,1)} %get-tuple-element.171), channel_id=1, source_target_pairs={{0,3},{1,4},{2,5},{3,6},{4,7},{5,8},{6,9},{7,10},{8,11},{9,12},{10... | collective-permute-start | bytes 786440 | tf_op jit(solution)/shard_map/ppermute | solution.py:16
  21.4 64.7 %collective-permute-start.1 = (bf16[512,256]{1,0:T(8,128)(2,1)}, bf16[512,256]{1,0:T(8,128)(2,1)}, u32[]{:S(2)}, u32[]{:S(2)}) collective-permute-start(bf16[512,256]{1,0:T(8,128)(2,1)} %get-tuple-element.167), channel_id=1, source_target_pairs={{0,2},{1,3},{2,4},{3,5},{4,6},{5,7},{6,8},{7,9},{8,10},{9,11},{10,... | collective-permute-start | bytes 786440 | tf_op jit(solution)/shard_map/ppermute | solution.py:16
  25.9 61.2 %collective-permute-start.2 = (bf16[512,256]{1,0:T(8,128)(2,1)}, bf16[512,256]{1,0:T(8,128)(2,1)}, u32[]{:S(2)}, u32[]{:S(2)}) collective-permute-start(bf16[512,256]{1,0:T(8,128)(2,1)} %get-tuple-element.168), channel_id=1, source_target_pairs={{0,1},{1,2},{2,3},{3,4},{4,5},{5,6},{6,7},{7,8},{8,9},{9,10},{10,1... | collective-permute-start | bytes 786440 | tf_op jit(solution)/shard_map/ppermute | solution.py:16
  28.4 59.7 %collective-permute-start.3 = (bf16[512,256]{1,0:T(8,128)(2,1)}, bf16[512,256]{1,0:T(8,128)(2,1)}, u32[]{:S(2)}, u32[]{:S(2)}) collective-permute-start(bf16[512,256]{1,0:T(8,128)(2,1)} %get-tuple-element.169), channel_id=1, source_target_pairs={{1,0},{2,1},{3,2},{4,3},{5,4},{6,5},{7,6},{8,7},{9,8},{10,9},{11,1... | collective-permute-start | bytes 786440 | tf_op jit(solution)/shard_map/ppermute | solution.py:16
  29.7 59.4 %collective-permute-start.4 = (bf16[512,256]{1,0:T(8,128)(2,1)}, bf16[512,256]{1,0:T(8,128)(2,1)}, u32[]{:S(2)}, u32[]{:S(2)}) collective-permute-start(bf16[512,256]{1,0:T(8,128)(2,1)} %get-tuple-element.170), channel_id=1, source_target_pairs={{2,0},{3,1},{4,2},{5,3},{6,4},{7,5},{8,6},{9,7},{10,8},{11,9},{12,... | collective-permute-start | bytes 786440 | tf_op jit(solution)/shard_map/ppermute | solution.py:16
  83.9 11.7 %collective-permute-start.5 = (bf16[512,256]{1,0:T(8,128)(2,1)}, bf16[512,256]{1,0:T(8,128)(2,1)S(1)}, u32[]{:S(2)}, u32[]{:S(2)}) collective-permute-start(bf16[512,256]{1,0:T(8,128)(2,1)} %get-tuple-element.166), channel_id=1, source_target_pairs={{3,0},{4,1},{5,2},{6,3},{7,4},{8,5},{9,6},{10,7},{11,8},{12,9},{13... | collective-permute-start | bytes 786440 | tf_op jit(solution)/shard_map/ppermute | solution.py:16
  95.7 1.4 copy-start.4
  100.7 1.0 copy-start.5
  101.9 4.1 copy-start.8
  102.1 7.4 %copy-start.3 = (bf16[27,512,256]{2,1,0:T(8,128)(2,1)}, bf16[27,512,256]{2,1,0:T(8,128)(2,1)S(1)}, u32[]{:S(2)}) copy-start(bf16[27,512,256]{2,1,0:T(8,128)(2,1)S(1)} %constant_dynamic-update-slice_fusion.7) | copy-start | bytes 21233668
  112.7 13.4 %collective-permute-start.6 = (bf16[512,256]{1,0:T(8,128)(2,1)S(1)}, bf16[512,256]{1,0:T(8,128)(2,1)S(1)}, u32[]{:S(2)}, u32[]{:S(2)}) collective-permute-start(bf16[512,256]{1,0:T(8,128)(2,1)S(1)} %get-tuple-element.186), channel_id=1, source_target_pairs={{0,3},{1,4},{2,5},{3,6},{4,7},{5,8},{6,9},{7,10},{8,11},{9,12},{10... | collective-permute-start | bytes 786440 | tf_op jit(solution)/shard_map/ppermute | solution.py:16
  116.7 10.9 %collective-permute-start.7 = (bf16[512,256]{1,0:T(8,128)(2,1)S(1)}, bf16[512,256]{1,0:T(8,128)(2,1)S(1)}, u32[]{:S(2)}, u32[]{:S(2)}) collective-permute-start(bf16[512,256]{1,0:T(8,128)(2,1)S(1)} %get-tuple-element.185), channel_id=1, source_target_pairs={{0,2},{1,3},{2,4},{3,5},{4,6},{5,7},{6,8},{7,9},{8,10},{9,11},{10,... | collective-permute-start | bytes 786440 | tf_op jit(solution)/shard_map/ppermute | solution.py:16
  120.4 8.9 %collective-permute-start.8 = (bf16[512,256]{1,0:T(8,128)(2,1)S(1)}, bf16[512,256]{1,0:T(8,128)(2,1)S(1)}, u32[]{:S(2)}, u32[]{:S(2)}) collective-permute-start(bf16[512,256]{1,0:T(8,128)(2,1)S(1)} %get-tuple-element.184), channel_id=1, source_target_pairs={{0,1},{1,2},{2,3},{3,4},{4,5},{5,6},{6,7},{7,8},{8,9},{9,10},{10,1... | collective-permute-start | bytes 786440 | tf_op jit(solution)/shard_map/ppermute | solution.py:16
  123.5 8.3 %collective-permute-start.9 = (bf16[512,256]{1,0:T(8,128)(2,1)S(1)}, bf16[512,256]{1,0:T(8,128)(2,1)S(1)}, u32[]{:S(2)}, u32[]{:S(2)}) collective-permute-start(bf16[512,256]{1,0:T(8,128)(2,1)S(1)} %get-tuple-element.183), channel_id=1, source_target_pairs={{1,0},{2,1},{3,2},{4,3},{5,4},{6,5},{7,6},{8,7},{9,8},{10,9},{11,1... | collective-permute-start | bytes 786440 | tf_op jit(solution)/shard_map/ppermute | solution.py:16
  124.8 12.5 %collective-permute-start.10 = (bf16[512,256]{1,0:T(8,128)(2,1)S(1)}, bf16[512,256]{1,0:T(8,128)(2,1)S(1)}, u32[]{:S(2)}, u32[]{:S(2)}) collective-permute-start(bf16[512,256]{1,0:T(8,128)(2,1)S(1)} %get-tuple-element.182), channel_id=1, source_target_pairs={{2,0},{3,1},{4,2},{5,3},{6,4},{7,5},{8,6},{9,7},{10,8},{11,9},{12,... | collective-permute-start | bytes 786440 | tf_op jit(solution)/shard_map/ppermute | solution.py:16
  126.1 15.3 %collective-permute-start.11 = (bf16[512,256]{1,0:T(8,128)(2,1)S(1)}, bf16[512,256]{1,0:T(8,128)(2,1)S(1)}, u32[]{:S(2)}, u32[]{:S(2)}) collective-permute-start(bf16[512,256]{1,0:T(8,128)(2,1)S(1)} %get-tuple-element.8), channel_id=1, source_target_pairs={{3,0},{4,1},{5,2},{6,3},{7,4},{8,5},{9,6},{10,7},{11,8},{12,9},{13... | collective-permute-start | bytes 786440 | tf_op jit(solution)/shard_map/ppermute | solution.py:16
  146.8 1.0 copy-start.9
  155.0 0.7 copy-start.1
  171.1 478.2 %reduce-scatter.3.cloned.1.call-start = ((), (), s32[]{:S(2)}) async-start(), calls=%async_computation.2 | async-start | bytes 8650752 | tf_op jit(solution)/shard_map/reduce_scatter | solution.py:70
  171.1 16.2 %collective-permute-start.12 = (bf16[512,256]{1,0:T(8,128)(2,1)}, bf16[512,256]{1,0:T(8,128)(2,1)S(1)}, u32[]{:S(2)}, u32[]{:S(2)}) collective-permute-start(bf16[512,256]{1,0:T(8,128)(2,1)} %get-tuple-element.179), channel_id=1, source_target_pairs={{0,3},{1,4},{2,5},{3,6},{4,7},{5,8},{6,9},{7,10},{8,11},{9,12},{10... | collective-permute-start | bytes 786440 | tf_op jit(solution)/shard_map/ppermute | solution.py:16
  173.3 15.6 %collective-permute-start.13 = (bf16[512,256]{1,0:T(8,128)(2,1)}, bf16[512,256]{1,0:T(8,128)(2,1)S(1)}, u32[]{:S(2)}, u32[]{:S(2)}) collective-permute-start(bf16[512,256]{1,0:T(8,128)(2,1)} %get-tuple-element.178), channel_id=1, source_target_pairs={{0,2},{1,3},{2,4},{3,5},{4,6},{5,7},{6,8},{7,9},{8,10},{9,11},{10,... | collective-permute-start | bytes 786440 | tf_op jit(solution)/shard_map/ppermute | solution.py:16
  183.4 6.5 collective-permute-start.14
  184.7 11.8 %collective-permute-start.15 = (bf16[512,256]{1,0:T(8,128)(2,1)}, bf16[512,256]{1,0:T(8,128)(2,1)S(1)}, u32[]{:S(2)}, u32[]{:S(2)}) collective-permute-start(bf16[512,256]{1,0:T(8,128)(2,1)} %get-tuple-element.176), channel_id=1, source_target_pairs={{1,0},{2,1},{3,2},{4,3},{5,4},{6,5},{7,6},{8,7},{9,8},{10,9},{11,1... | collective-permute-start | bytes 786440 | tf_op jit(solution)/shard_map/ppermute | solution.py:16
  186.0 20.2 %collective-permute-start.16 = (bf16[512,256]{1,0:T(8,128)(2,1)}, bf16[512,256]{1,0:T(8,128)(2,1)S(1)}, u32[]{:S(2)}, u32[]{:S(2)}) collective-permute-start(bf16[512,256]{1,0:T(8,128)(2,1)} %get-tuple-element.175), channel_id=1, source_target_pairs={{2,0},{3,1},{4,2},{5,3},{6,4},{7,5},{8,6},{9,7},{10,8},{11,9},{12,... | collective-permute-start | bytes 786440 | tf_op jit(solution)/shard_map/ppermute | solution.py:16
  187.3 18.9 %collective-permute-start.17 = (bf16[512,256]{1,0:T(8,128)(2,1)}, bf16[512,256]{1,0:T(8,128)(2,1)S(1)}, u32[]{:S(2)}, u32[]{:S(2)}) collective-permute-start(bf16[512,256]{1,0:T(8,128)(2,1)} %get-tuple-element.174), channel_id=1, source_target_pairs={{3,0},{4,1},{5,2},{6,3},{7,4},{8,5},{9,6},{10,7},{11,8},{12,9},{13... | collective-permute-start | bytes 786440 | tf_op jit(solution)/shard_map/ppermute | solution.py:16
  207.5 1.0 copy-start.2
  264.1 453.9 %all-reduce.3.cloned.1.call-start = ((), (), s32[]{:S(2)}) async-start(), calls=%async_computation.4 | async-start | bytes 1048576 | tf_op jit(solution)/shard_map/psum | solution.py:76
Sparse Core Ops, SparseCore 0:
  171.2 245.9 reduce-scatter.4
  421.8 227.4 reduce-scatter.2
  651.7 66.3 all-reduce.2
where the time goes:
time: 731 us; the launch traced here: 728 us
  waiting for transfers between devices  490 us (67%)
  local copies, waits for them, and re-layouts  73.4 us (10%)
  between operations  64.3 us (9%)
  starting transfers between devices  49.4 us (7%)
  matrix products  31.6 us (4%)
  other arithmetic  19 us (3%)
    reduce_scatter x2, waiting for transfers between devices, reduce_grads(): lax.psum_scatter(jnp.einsum('kvc,vd->ckd', wins, grad, preferred_element_...  385 us
    psum x1, waiting for transfers between devices, reduce_grads(): return lax.psum(mine, 'dp')  68.8 us
    ppermute x18, starting transfers between devices, passed_along(): return lax.ppermute(block, axis, route)  49.2 us
    ppermute x18, waiting for transfers between devices, passed_along(): return lax.ppermute(block, axis, route)  36.5 us
    unnamed x117, local copies, waits for them, and re-layouts  35.2 us
    dot_general x2, matrix products, reduce_grads(): jnp.einsum('kvc,vd->ckd', wins, grad, preferred_element_type=jnp.float32)  20.9 us
    transpose x2, local copies, waits for them, and re-layouts, reduce_grads(): jnp.einsum('kvc,vd->ckd', wins, grad, preferred_element_type=jnp.float32)  20.7 us
  transfers between devices with their start and end apart: 21, of which 11 were waited for; matrix products, arithmetic and copies ran while one was open for 9% of the time, Pallas kernels for 0%

commit v1 on v0

v1 whole, which is shorter than its diff:
```python
import jax
import jax.numpy as jnp
import numpy as np
from jax import lax
from jax.experimental import pallas as pl
from jax.experimental.pallas import tpu as pltpu
from jax.sharding import PartitionSpec as P

E = 8
VOX = E**3
C = 256
NX, NY, NZ = 4, 4, 8
BRICKS = NX * NZ
DISTANCES = (-3, -2, -1, 1, 2, 3)
PAY = E * E
OWN = VOX
ROWS = VOX + 6 * PAY
KP = 28
PIECE = KP * 8
SHARE = PIECE // 4
LANES = 128
F32 = jnp.float32
BF16 = jnp.bfloat16
MESH = pl.DeviceIdType.MESH


def offset_index(shift):
    number = (shift[0] + 1) * 9 + (shift[1] + 1) * 3 + (shift[2] + 1)
    return None if number == 13 else (number if number < 13 else number - 1)


def padded_table():
    table = np.zeros((3, 10, 10, 8, 128), np.float32)
    for oc in range(3):
        for a in range(10):
            for b in range(10):
                for c in range(8):
                    at = (a, b, c + oc)
                    shift = [-1 if t == 0 else (1 if t == 9 else 0) for t in at]
                    free = [t - 1 for t, m in zip(at, shift) if m == 0]
                    q = offset_index(shift)
                    line = table[oc, a, b, c]
                    if q is None:
                        line[27] = free[0]
                        line[26] = free[1] * 8 + free[2]
                    else:
                        line[q] = 1
                        row = 0
                        for t in free:
                            row = row * 8 + t
                        line[26] = row
    return table.reshape(3 * 800, 128)


def payload_table():
    hi = np.zeros((PAY, 128), np.float32)
    lo = np.zeros((PAY, 128), np.float32)
    for a in (-1, 0, 1):
        for b in (-1, 0, 1):
            for c in (-1, 0, 1):
                shift = (a, b, c)
                q = offset_index(shift)
                if q is None:
                    continue
                n_free = sum(t == 0 for t in shift)
                for r in range(8**n_free):
                    rest, at = r, [0, 0, 0]
                    for dim in (2, 1, 0):
                        if shift[dim] == 0:
                            at[dim] = rest % 8
                            rest //= 8
                        else:
                            at[dim] = 7 if shift[dim] == 1 else 0
                    hi[r, q] = at[0] + 1
                    lo[r, q] = at[1] * 8 + at[2]
    return np.concatenate([hi, lo], axis=1)


def kernel(
    feat, occ, nbr, send, cot, w1_hbm, w2_hbm, qtab, ptab,
    out,
    w1, w2, nbrv, occb, sel, oh, um, uh, ug, hsend, win_m, win_h, pre, grads,
    psend, precv, asend, arecv, zsend, zrecv, bsend, brecv, gath,
    wsem, hs, hr, ps, pr, as_, ar, zs, zr, bs, br, gs, gr,
):
    d = lax.axis_index("dp")
    s = lax.axis_index("space")
    core = lax.rem(d, 2)
    y = d // 2
    x = lax.rem(s, NX)
    z = s // NX
    not_core = 1 - core
    pa = x * not_core + y * core
    pb = y * not_core + x * core

    def a_dev(j):
        return (d * not_core + (2 * j + core) * core, (z * NX + j) * not_core + s * core)

    def b_dev(j):
        return ((2 * j + core) * not_core + d * core, s * not_core + (z * NX + j) * core)

    def z_dev(j):
        return (d, j * NX + x)

    def group_dev(dy, dc):
        return (lax.rem(y + dy, NY) * 2 + lax.rem(core + dc, 2), s)

    relations = [(dy, dc) for dy in range(NY) for dc in range(2) if dy or dc]

    load1 = pltpu.make_async_copy(w1_hbm, w1, wsem.at[0])
    load1.start()
    load2 = pltpu.make_async_copy(w2_hbm, w2, wsem.at[1])
    load2.start()

    barrier = pltpu.get_barrier_semaphore()
    partners = [group_dev(dy, dc) for dy, dc in relations]
    partners += [(d, z * NX + lax.rem(x + j, NX)) for j in (1, 2, 3)]
    partners += [z_dev(lax.rem(z + 1, NZ)), z_dev(lax.rem(z + NZ - 1, NZ))]
    partners += [(d, lax.rem(s + t + BRICKS, BRICKS)) for t in DISTANCES]
    for partner in partners:
        pl.semaphore_signal(barrier, inc=1, device_id=partner, device_id_type=MESH)

    pending = []

    def push(src, dst, send_sem, recv_sem, dev):
        copy = pltpu.make_async_remote_copy(
            src_ref=src, dst_ref=dst, send_sem=send_sem, recv_sem=recv_sem,
            device_id=dev, device_id_type=MESH,
        )
        copy.start()
        pending.append(copy)
        return copy

    occ_row = jnp.broadcast_to(occ[...].astype(F32), (LANES, VOX))
    for j in range(VOX // LANES):
        occb[pl.ds(j * LANES, LANES), :] = occ_row[:, j * LANES : (j + 1) * LANES].T

    def occupied():
        return jnp.concatenate([occb[...], occb[...]], axis=1)

    um[pl.ds(0, OWN), :] = (feat[...].astype(F32) * occupied()).astype(BF16)

    nbrv[...] = jnp.full((1, 128), -1, jnp.int32)
    nbrv[:, 0:26] = nbr[...]
    slots = nbrv[...]
    scale = jnp.where(lax.broadcasted_iota(jnp.int32, (256, 128), 0) < 128, 64.0, 1.0).astype(BF16)
    lane = lax.broadcasted_iota(jnp.int32, (PAY, 128), 1)
    for t in range(6):
        flag = send[0, t].astype(F32)
        chosen = jnp.where(slots == t, flag, 0.0)
        rows = ptab[...] * jnp.concatenate([chosen, chosen], axis=1)
        voxel = jnp.dot(rows.astype(BF16), scale, preferred_element_type=F32).astype(jnp.int32)
        for j in range(VOX // LANES):
            hit = voxel == lane + (64 + j * LANES)
            sel[pl.ds(t * PAY, PAY), pl.ds(j * LANES, LANES)] = jnp.where(hit, 1.0, 0.0).astype(BF16)

    pl.semaphore_wait(barrier, len(partners))

    def send_halo(which, field):
        packed = jnp.dot(sel[...], field[pl.ds(0, OWN), :], preferred_element_type=F32)
        hsend[which] = packed.astype(BF16)
        return [
            push(
                hsend.at[which, pl.ds(t * PAY, PAY)],
                field.at[pl.ds(OWN + (5 - t) * PAY, PAY)],
                hs.at[which, t],
                hr.at[which, 5 - t],
                (d, lax.rem(s + DISTANCES[t] + BRICKS, BRICKS)),
            )
            for t in range(6)
        ]

    sent = send_halo(0, um)

    distance = jnp.where(slots < 3, slots - 3, slots - 2)
    other = s + distance
    present = (slots >= 0) & (slots < 6) & (other >= 0) & (other < BRICKS)
    base = jnp.where(present, 64 * (8 + slots), 64 * 32).astype(F32)
    lane1 = lax.broadcasted_iota(jnp.int32, (1, 128), 1)
    base = jnp.where(lane1 < 26, base, jnp.where(lane1 == 26, 1.0, jnp.where(lane1 == 27, 64.0, 0.0)))
    ones = jnp.ones((128, 128), BF16)

    def lay(i, carry):
        at = pl.multiple_of(i * 80, 16)
        rows = qtab[pl.ds(at, 80), :].astype(F32) * base
        source = jnp.dot(rows.astype(BF16), ones, preferred_element_type=F32).astype(jnp.int32)
        lanes80 = lax.broadcasted_iota(jnp.int32, (80, 128), 1)
        for j in range(ROWS // LANES):
            hit = source == lanes80 + j * LANES
            oh[pl.ds(at, 80), pl.ds(j * LANES, LANES)] = jnp.where(hit, 1.0, 0.0).astype(BF16)
        return carry

    lax.fori_loop(0, 30, lay, 0)

    def build_windows(field, win):
        def one(oc, carry):
            for half in range(2):
                rows = oh[pl.ds(pl.multiple_of(oc * 800 + half * 400, 16), 400), :]
                padded = jnp.dot(rows, field[...], preferred_element_type=F32).reshape(5, 80, C)
                for ob in range(3):
                    part = padded[:, ob * 8 : ob * 8 + 64].reshape(320, C).astype(BF16)
                    lanes = pl.ds(pl.multiple_of((ob * 3 + oc) * C, C), C)
                    win[pl.ds(half * 320, 320), lanes] = part
            return carry

        lax.fori_loop(0, 3, one, 0)

    def conv(win, weight):
        for m in range(2):
            acc = jnp.zeros((256, C), F32)
            for oa in range(3):
                acc = acc + jnp.dot(
                    win[pl.ds(oa * 64 + m * 256, 256), :],
                    weight[pl.ds(oa * 9 * C, 9 * C), :],
                    preferred_element_type=F32,
                )
            yield m, acc

    def slope(value):
        sig = jax.nn.sigmoid(value)
        return sig * (1.0 + value * (1.0 - sig))

    def half_occ(m):
        part = occb[pl.ds(m * 256, 256), :]
        return jnp.concatenate([part, part], axis=1)

    for copy in sent:
        copy.wait_recv()
    build_windows(um, win_m)
    load1.wait()
    for m, acc in conv(win_m, w1):
        value = acc * half_occ(m)
        pre[pl.ds(m * 256, 256), :] = value
        uh[pl.ds(m * 256, 256), :] = (value * jax.nn.sigmoid(value)).astype(BF16)
    sent = send_halo(1, uh)
    for copy in sent:
        copy.wait_recv()
    build_windows(uh, win_h)
    load2.wait()
    for m, acc in conv(win_h, w2):
        rows = pl.ds(m * 256, 256)
        value = acc * half_occ(m) + um[rows, :].astype(F32)
        ug[rows, :] = (cot[rows, :].astype(F32) * slope(value) * half_occ(m)).astype(BF16)
    sent = send_halo(2, ug)

    def weight_grad(g, win, grad):
        def one(k, carry):
            view = win[
                pl.ds(pl.multiple_of((k // 9) * 64, 64), VOX),
                pl.ds(pl.multiple_of(lax.rem(k, 9) * C, C), C),
            ]
            res = lax.dot_general(view, grad[pl.ds(0, OWN), :], (((0,), (0,)), ((), ())), preferred_element_type=F32)
            res = res.reshape(NZ, NX, 8, C)
            ky = k // 7
            for xx in range(NX):
                grads[g, 0, xx, :, pl.ds(pl.multiple_of(k * 8, 8), 8), :] = res[:, xx, :, :LANES]
                at = pl.multiple_of(xx * SHARE + lax.rem(k, 7) * 8, 8)
                grads[g, 1, ky, :, pl.ds(at, 8), :] = res[:, xx, :, LANES:]
            return carry

        lax.fori_loop(0, 27, one, 0)
        blank = jnp.zeros((NZ, 8, LANES), F32)
        for xx in range(NX):
            grads[g, 0, xx, :, pl.ds(27 * 8, 8), :] = blank
            grads[g, 1, 3, :, pl.ds(xx * SHARE + 48, 8), :] = blank

    def pair_start(g):
        copies = []
        for j, step in enumerate((2, 1, 3, 0)):
            block = lax.rem(pb + step, 4)

            def cast(i, carry):
                psend[g, block, i] = grads[g, not_core, block, i].astype(BF16)
                return carry

            lax.fori_loop(0, NZ, cast, 0)
            copies.append(
                push(psend.at[g, block], precv.at[g, block], ps.at[g, j], pr.at[g, j], (d + not_core - core, s))
            )
        return copies

    right_a, left_a = a_dev(lax.rem(pa + 1, 4)), a_dev(lax.rem(pa + 3, 4))

    def a_push(g, slot, dev):
        return push(asend.at[g, slot], arecv.at[g, slot], as_.at[g, slot], ar.at[g, slot], dev)

    def ring_a_first(g, pairs):
        opposite, right, left = lax.rem(pa + 2, 4), lax.rem(pa + 1, 4), lax.rem(pa + 3, 4)
        copies = [None] * 6

        def fold(block):
            def add(i, carry):
                grads[g, core, block, i] = grads[g, core, block, i] + precv[g, block, i].astype(F32)
                return carry

            lax.fori_loop(0, NZ, add, 0)

        def stage(slot, block, lo):
            def cast(i, carry):
                asend[g, slot, i] = grads[g, core, block, lo + i].astype(BF16)
                return carry

            lax.fori_loop(0, 4, cast, 0)

        pairs[0].wait_recv()
        fold(opposite)
        stage(0, opposite, 0)
        copies[0] = a_push(g, 0, right_a)
        stage(1, opposite, 4)
        copies[1] = a_push(g, 1, left_a)
        pairs[1].wait_recv()
        fold(right)
        stage(2, right, 4)
        copies[2] = a_push(g, 2, right_a)
        pairs[2].wait_recv()
        fold(left)
        stage(3, left, 0)
        copies[3] = a_push(g, 3, left_a)
        pairs[3].wait_recv()
        fold(pa)
        return copies

    def ring_a_second(g, copies):
        right, left = lax.rem(pa + 1, 4), lax.rem(pa + 3, 4)
        for slot, block, lo, dev in ((4, right, 0, right_a), (5, left, 4, left_a)):
            copies[slot - 4].wait_recv()

            def add(i, carry):
                total = grads[g, core, block, lo + i] + arecv[g, slot - 4, i].astype(F32)
                asend[g, slot, i] = total.astype(BF16)
                return carry

            lax.fori_loop(0, 4, add, 0)
            copies[slot] = a_push(g, slot, dev)

    def ring_a_last(g, copies):
        for slot in (2, 3, 4, 5):
            copies[slot].wait_recv()

        def add(i, carry):
            low = arecv[g, 4, i].astype(F32) + arecv[g, 3, i].astype(F32)
            grads[g, core, pa, i] = grads[g, core, pa, i] + low
            high = arecv[g, 2, i].astype(F32) + arecv[g, 5, i].astype(F32)
            grads[g, core, pa, i + 4] = grads[g, core, pa, i + 4] + high
            return carry

        lax.fori_loop(0, 4, add, 0)

    sides = (z_dev(lax.rem(z + 1, NZ)), z_dev(lax.rem(z + NZ - 1, NZ)))
    HALF = PIECE // 2

    def ring_z_step(g, step, before):
        copies = []
        for way in range(2):
            hop = 4 - step
            block = lax.rem(z + (hop if way == 0 else NZ - hop), NZ)
            mine = pl.ds(way * HALF, HALF)
            if step == 0:
                zsend[g, way, 0, mine, :] = grads[g, core, pa, block, mine, :].astype(BF16)
                part = mine
            else:
                before[way].wait_recv()
                if step == 1:
                    rest = pl.ds((1 - way) * HALF, HALF)
                    zsend[g, way, 1, rest, :] = grads[g, core, pa, block, rest, :].astype(BF16)
                    total = grads[g, core, pa, block, mine, :] + zrecv[g, way, 0, mine, :].astype(F32)
                    zsend[g, way, 1, mine, :] = total.astype(BF16)
                else:
                    total = grads[g, core, pa, block] + zrecv[g, way, step - 1].astype(F32)
                    zsend[g, way, step] = total.astype(BF16)
                part = pl.ds(0, PIECE)
            copies.append(
                push(
                    zsend.at[g, way, step, part],
                    zrecv.at[g, way, step, part],
                    zs.at[g, way, step],
                    zr.at[g, way, step],
                    sides[way],
                )
            )
        return copies

    def ring_b_start(g, before):
        for copy in before:
            copy.wait_recv()
        total = grads[g, core, pa, z] + (zrecv[g, 0, 3].astype(F32) + zrecv[g, 1, 3].astype(F32))
        bsend[g] = total
        copies = []
        for j in (1, 2, 3):
            to = lax.rem(pb + j, 4)
            copies.append(
                push(
                    bsend.at[g, pl.ds(pl.multiple_of(to * SHARE, 8), SHARE)],
                    brecv.at[g, j - 1],
                    bs.at[g, j - 1],
                    br.at[g, j - 1],
                    b_dev(to),
                )
            )
        return copies

    def gather_start(g, before):
        for copy in before:
            copy.wait_recv()
        total = bsend[g, pl.ds(pl.multiple_of(pb * SHARE, 8), SHARE), :]
        for j in range(3):
            total = total + brecv[g, j]
        gath[g, y, core] = total
        return [
            push(gath.at[g, y, core], gath.at[g, y, core], gs.at[g, n], gr.at[g, n], group_dev(dy, dc))
            for n, (dy, dc) in enumerate(relations)
        ]

    weight_grad(0, win_h, ug)
    pairs_two = pair_start(0)

    for copy in sent:
        copy.wait_recv()
    build_windows(ug, win_h)
    ring_two = ring_a_first(0, pairs_two)
    for m in range(2):
        acc = jnp.zeros((256, C), F32)
        for oa in range(3):
            weights = jnp.concatenate([w2[pl.ds((26 - oa * 9 - j) * C, C), :] for j in range(9)], axis=1)
            acc = acc + lax.dot_general(
                win_h[pl.ds(oa * 64 + m * 256, 256), :],
                weights,
                (((1,), (1,)), ((), ())),
                preferred_element_type=F32,
            )
        rows = pl.ds(m * 256, 256)
        uh[rows, :] = (acc * slope(pre[rows, :]) * half_occ(m)).astype(BF16)
    ring_a_second(0, ring_two)

    weight_grad(1, win_m, uh)
    pairs_one = pair_start(1)
    ring_a_last(0, ring_two)
    steps = ring_z_step(0, 0, None)
    ring_one = ring_a_first(1, pairs_one)
    steps = ring_z_step(0, 1, steps)
    ring_a_second(1, ring_one)
    steps = ring_z_step(0, 2, steps)
    steps = ring_z_step(0, 3, steps)
    steps = ring_b_start(0, steps)
    done_two = gather_start(0, steps)
    ring_a_last(1, ring_one)
    steps = None
    for step in range(4):
        steps = ring_z_step(1, step, steps)
    steps = ring_b_start(1, steps)
    done_one = gather_start(1, steps)
    for copy in done_two + done_one:
        copy.wait_recv()
    out[...] = gath[...]
    for copy in pending:
        copy.wait_send()


def local(features, occupancy, nbr_slots, send_mask, cotangent, weight_one, weight_two):
    vmem = pl.BlockSpec(memory_space=pltpu.VMEM)
    smem = pl.BlockSpec(memory_space=pltpu.SMEM)
    hbm = pl.BlockSpec(memory_space=pl.ANY)
    dma = pltpu.SemaphoreType.DMA
    res = pl.pallas_call(
        kernel,
        out_shape=jax.ShapeDtypeStruct((2, NY, 2, SHARE, LANES), F32),
        in_specs=[vmem, vmem, vmem, smem, vmem, hbm, hbm, vmem, vmem],
        out_specs=vmem,
        scratch_shapes=[
            pltpu.VMEM((27 * C, C), BF16),
            pltpu.VMEM((27 * C, C), BF16),
            pltpu.VMEM((1, 128), jnp.int32),
            pltpu.VMEM((VOX, LANES), F32),
            pltpu.VMEM((6 * PAY, VOX), BF16),
            pltpu.VMEM((2400, ROWS), BF16),
            pltpu.VMEM((ROWS, C), BF16),
            pltpu.VMEM((ROWS, C), BF16),
            pltpu.VMEM((ROWS, C), BF16),
            pltpu.VMEM((3, 6 * PAY, C), BF16),
            pltpu.VMEM((640, 9 * C), BF16),
            pltpu.VMEM((640, 9 * C), BF16),
            pltpu.VMEM((VOX, C), F32),
            pltpu.VMEM((2, 2, 4, NZ, PIECE, LANES), F32),
            pltpu.VMEM((2, 4, NZ, PIECE, LANES), BF16),
            pltpu.VMEM((2, 4, NZ, PIECE, LANES), BF16),
            pltpu.VMEM((2, 6, 4, PIECE, LANES), BF16),
            pltpu.VMEM((2, 6, 4, PIECE, LANES), BF16),
            pltpu.VMEM((2, 2, 4, PIECE, LANES), BF16),
            pltpu.VMEM((2, 2, 4, PIECE, LANES), BF16),
            pltpu.VMEM((2, PIECE, LANES), F32),
            pltpu.VMEM((2, 3, SHARE, LANES), F32),
            pltpu.VMEM((2, NY, 2, SHARE, LANES), F32),
            dma((2,)),
            dma((3, 6)),
            dma((3, 6)),
            dma((2, 4)),
            dma((2, 4)),
            dma((2, 6)),
            dma((2, 6)),
            dma((2, 2, 4)),
            dma((2, 2, 4)),
            dma((2, 3)),
            dma((2, 3)),
            dma((2, 7)),
            dma((2, 7)),
        ],
        compiler_params=pltpu.CompilerParams(
            collective_id=0, has_side_effects=True, vmem_limit_bytes=60 * 1024 * 1024
        ),
    )(
        features.reshape(VOX, C),
        occupancy.reshape(1, VOX),
        nbr_slots.reshape(1, 26),
        send_mask.reshape(1, 6),
        cotangent.reshape(VOX, C),
        weight_one.reshape(27 * C, C),
        weight_two.reshape(27 * C, C),
        jnp.asarray(padded_table(), BF16),
        jnp.asarray(payload_table(), F32),
    )
    res = res.reshape(2, NY, 2, 7, 8, LANES).transpose(0, 4, 1, 3, 2, 5).reshape(2, 8, KP, C)[:, :, :27]
    return res[1], res[0]


def solution(mesh):
    in_specs = (
        P("dp", "space", None, None),
        P("dp", "space", None),
        P("dp", "space", None),
        P("dp", "space", None),
        P("dp", "space", None, None),
        P(),
        P(),
    )
    out_specs = (P("space", None, None), P("space", None, None))
    return jax.shard_map(local, mesh=mesh, in_specs=in_specs, out_specs=out_specs, check_vma=False)
```

time: 731 us -> 101 us (0.14)
  waiting for transfers between devices: 490 us -> 0 us
  Pallas kernels: 0 us -> 98.1 us
  local copies, waits for them, and re-layouts: 73.4 us -> 1.84 us
  between operations: 64.3 us -> 0.65 us
  starting transfers between devices: 49.4 us -> 0 us
  matrix products: 31.6 us -> 0 us
  other arithmetic: 19 us -> 0 us
    reduce_scatter x2 -> x0, waiting for transfers between devices: 385 us -> none  [reduce_grads(): lax.psum_scatter(jnp.einsum('kvc,vd->ckd', wins, grad, preferred_element_...]
    pallas_call x0 -> x1, Pallas kernels: none -> 98.1 us  [local(): pl.pallas_call(kernel, out_shape=jax.ShapeDtypeStruct((2, NY, 2, SHARE, L...]
    psum x1 -> x0, waiting for transfers between devices: 68.8 us -> none  [reduce_grads(): return lax.psum(mine, 'dp')]
    ppermute x18 -> x0, starting transfers between devices: 49.2 us -> none  [passed_along(): return lax.ppermute(block, axis, route)]
    ppermute x18 -> x0, waiting for transfers between devices: 36.5 us -> none  [passed_along(): return lax.ppermute(block, axis, route)]
    unnamed x117 -> x0, local copies, waits for them, and re-layouts: 35.2 us -> none
    dot_general x4 -> x0, matrix products: 31.6 us -> none  [the longest x2 20.9 us: reduce_grads(): jnp.einsum('kvc,vd->ckd', wins, grad, preferred_element_type=jnp.float32)]
    transpose x2 -> x1, local copies, waits for them, and re-layouts: 20.7 us -> 1.05 us  [local(): res.reshape(2, NY, 2, 7, 8, LANES).transpose(0, 4, 1, 3, 2, 5)]
  transfers between devices with their start and end apart: 21 -> 0, of which waited for: 11 -> 0; matrix products, arithmetic and copies ran while one was open for 9% -> 0% of each run, Pallas kernels for 0% -> 0%
where the time goes in v1:
time: 101 us
  Pallas kernels  98.1 us (97%)
  local copies, waits for them, and re-layouts  1.84 us (2%)
    pallas_call x1, Pallas kernels, local(): pl.pallas_call(kernel, out_shape=jax.ShapeDtypeStruct((2, NY, 2, SHARE, L...  98.1 us

profile of v1, /device:TPU:1, one launch (start us, length us, event | category | flops | bytes accessed | tf_op | source)
XLA Modules:
  0.0 100.6 jit_solution(8599720390750424700)
XLA Ops:
  0.6 98.1 %shard_map.104 = f32[2,4,2,56,128]{4,3,2,1,0:T(8,128)} custom-call(bf16[512,256]{1,0:T(8,128)(2,1)} %bitcast.19, s32[1,512]{1,0:T(1,128)} %bitcast.21, s32[1,26]{1,0:T(1,128)} %bitcast.22, s32[1,6]{1,0:T(1,128)} %bitcast.23, bf16[512,256]{1,0:T(8,128)(2,1)} %bitcast.20, bf16[6912,256]{1,0:T(8,128)(2,1)} %bitcast.15, bf16[6912,256]{1,0:T(8,128)(2,1)} %bitcast.16, ...), custom_call_target="tpu_custom_call" | custom-call | tf_op jit(solution)/shard_map/pallas_call | solution.py:464
  98.7 1.1 %copy.11 = f32[2,8,4,7,2,128]{5,1,4,3,2,0:T(8,128)S(1)} copy(f32[2,8,4,7,2,128]{5,1,3,4,2,0:T(8,128)} %bitcast.17) | data formatting | bytes 917504 | tf_op jit(solution)/shard_map/transpose | solution.py:521
  99.8 0.8 slice_bitcast_fusion

commit v2 on v1

v2 whole, which is shorter than its diff:
```python
import jax
import jax.numpy as jnp
import numpy as np
from jax import lax
from jax.experimental import pallas as pl
from jax.experimental.pallas import tpu as pltpu
from jax.sharding import PartitionSpec as P

E = 8
VOX = E**3
C = 256
NX, NY, NZ = 4, 4, 8
BRICKS = NX * NZ
DISTANCES = (-3, -2, -1, 1, 2, 3)
PAY = E * E
OWN = VOX
ROWS = VOX + 6 * PAY
KP = 28
UNITS = 14
UNROLL = 4
FLOWS = ((0, 6), (6, 4), (10, 2), (12, 2))
ROWS_ALL = UNITS * 4 * 8
LANES = 128
F32 = jnp.float32
BF16 = jnp.bfloat16
MESH = pl.DeviceIdType.MESH


def offset_index(shift):
    number = (shift[0] + 1) * 9 + (shift[1] + 1) * 3 + (shift[2] + 1)
    return None if number == 13 else (number if number < 13 else number - 1)


def padded_table():
    table = np.zeros((3, 10, 10, 8, 128), np.float32)
    for oc in range(3):
        for a in range(10):
            for b in range(10):
                for c in range(8):
                    at = (a, b, c + oc)
                    shift = [-1 if t == 0 else (1 if t == 9 else 0) for t in at]
                    free = [t - 1 for t, m in zip(at, shift) if m == 0]
                    q = offset_index(shift)
                    line = table[oc, a, b, c]
                    if q is None:
                        line[27] = free[0]
                        line[26] = free[1] * 8 + free[2]
                    else:
                        line[q] = 1
                        row = 0
                        for t in free:
                            row = row * 8 + t
                        line[26] = row
    return table.reshape(3 * 800, 128)


def payload_table():
    hi = np.zeros((PAY, 128), np.float32)
    lo = np.zeros((PAY, 128), np.float32)
    for a in (-1, 0, 1):
        for b in (-1, 0, 1):
            for c in (-1, 0, 1):
                shift = (a, b, c)
                q = offset_index(shift)
                if q is None:
                    continue
                n_free = sum(t == 0 for t in shift)
                for r in range(8**n_free):
                    rest, at = r, [0, 0, 0]
                    for dim in (2, 1, 0):
                        if shift[dim] == 0:
                            at[dim] = rest % 8
                            rest //= 8
                        else:
                            at[dim] = 7 if shift[dim] == 1 else 0
                    hi[r, q] = at[0] + 1
                    lo[r, q] = at[1] * 8 + at[2]
    return np.concatenate([hi, lo], axis=1)


def kernel(
    feat_hbm, occ, nbr, send, cot_hbm, w1_hbm, w2_hbm, qtab_hbm, ptab_hbm,
    out,
    feat, cot, qtab, ptab, w1, w2, nbrv, occb, sel, oh, um, uh, ug, hsend, win_m, win_h, tm, th, gpad, pre, grads,
    psend, precv, asend, arecv, zsend, zrecv, gath,
    wsem, hs, hr, ps, pr, as_, ar, zs, zr, gs, gr,
):
    d = lax.axis_index("dp")
    s = lax.axis_index("space")
    core = lax.rem(d, 2)
    y = d // 2
    x = lax.rem(s, NX)
    z = s // NX
    not_core = 1 - core
    pa = x * not_core + y * core
    pb = y * not_core + x * core

    near_x = [x] + [lax.rem(x + j, NX) for j in range(1, NX)]
    near_y = [y] + [lax.rem(y + j, NY) for j in range(1, NY)]
    near_z = [z] + [lax.rem(z + j, NZ) for j in range(1, NZ)]
    near_a = [i * not_core + j * core for i, j in zip(near_x, near_y)]
    near_b = [j * not_core + i * core for i, j in zip(near_x, near_y)]
    row_y = [2 * j + core for j in near_y]
    ring_dev = [(d * not_core + row_y[j] * core, z * NX + (near_x[j] * not_core + x * core)) for j in range(4)]
    b_dp = [row_y[j] * not_core + d * core for j in range(4)]
    b_sp = [x * not_core + near_x[j] * core for j in range(4)]
    row_z = [j * NX for j in near_z]

    def plane_dev(j):
        return (b_dp[j % 4], row_z[j // 4] + b_sp[j % 4])

    def group_dev(dy, dc):
        return (2 * near_y[dy] + (not_core if dc else core), s)

    relations = [(dy, dc) for dy in range(NY) for dc in range(2) if dy or dc]

    loads = []
    for n, (src, dst) in enumerate(
        ((ptab_hbm, ptab), (feat_hbm, feat), (qtab_hbm, qtab), (w1_hbm, w1), (cot_hbm, cot), (w2_hbm, w2))
    ):
        loads.append(pltpu.make_async_copy(src, dst, wsem.at[n]))
        loads[-1].start()

    barrier = pltpu.get_barrier_semaphore()
    partners = [group_dev(dy, dc) for dy, dc in relations]
    partners += [ring_dev[j] for j in (1, 2, 3)]
    partners += [plane_dev(j) for j in range(1, 32)]
    partners += [(d, lax.rem(s + t + BRICKS, BRICKS)) for t in DISTANCES]
    for partner in partners:
        pl.semaphore_signal(barrier, inc=1, device_id=partner, device_id_type=MESH)

    pending = []

    def push(src, dst, send_sem, recv_sem, dev):
        copy = pltpu.make_async_remote_copy(
            src_ref=src, dst_ref=dst, send_sem=send_sem, recv_sem=recv_sem,
            device_id=dev, device_id_type=MESH,
        )
        copy.start()
        pending.append(copy)
        return copy

    occ_row = jnp.broadcast_to(occ[...].astype(F32), (LANES, VOX))
    for j in range(VOX // LANES):
        occb[pl.ds(j * LANES, LANES), :] = occ_row[:, j * LANES : (j + 1) * LANES].T

    def occupied():
        return jnp.concatenate([occb[...], occb[...]], axis=1)

    loads[1].wait()
    um[pl.ds(0, OWN), :] = (feat[...].astype(F32) * occupied()).astype(BF16)

    nbrv[...] = jnp.full((1, 128), -1, jnp.int32)
    nbrv[:, 0:26] = nbr[...]
    slots = nbrv[...]
    scale = jnp.where(lax.broadcasted_iota(jnp.int32, (256, 128), 0) < 128, 64.0, 1.0).astype(BF16)
    lane = lax.broadcasted_iota(jnp.int32, (PAY, 128), 1)
    loads[0].wait()
    for t in range(6):
        flag = send[0, t].astype(F32)
        chosen = jnp.where(slots == t, flag, 0.0)
        rows = ptab[...] * jnp.concatenate([chosen, chosen], axis=1)
        voxel = jnp.dot(rows.astype(BF16), scale, preferred_element_type=F32).astype(jnp.int32)
        for j in range(VOX // LANES):
            hit = voxel == lane + (64 + j * LANES)
            sel[pl.ds(t * PAY, PAY), pl.ds(j * LANES, LANES)] = jnp.where(hit, 1.0, 0.0).astype(BF16)

    pl.semaphore_wait(barrier, len(partners))

    def send_halo(which, field):
        packed = jnp.dot(sel[...], field[pl.ds(0, OWN), :], preferred_element_type=F32)
        hsend[which] = packed.astype(BF16)
        return [
            push(
                hsend.at[which, pl.ds(t * PAY, PAY)],
                field.at[pl.ds(OWN + (5 - t) * PAY, PAY)],
                hs.at[which, t],
                hr.at[which, 5 - t],
                (d, lax.rem(s + DISTANCES[t] + BRICKS, BRICKS)),
            )
            for t in range(6)
        ]

    sent = send_halo(0, um)

    distance = jnp.where(slots < 3, slots - 3, slots - 2)
    other = s + distance
    present = (slots >= 0) & (slots < 6) & (other >= 0) & (other < BRICKS)
    base = jnp.where(present, 64 * (8 + slots), 64 * 32).astype(F32)
    lane1 = lax.broadcasted_iota(jnp.int32, (1, 128), 1)
    base = jnp.where(lane1 < 26, base, jnp.where(lane1 == 26, 1.0, jnp.where(lane1 == 27, 64.0, 0.0)))
    ones = jnp.ones((128, 128), BF16)

    def lay(i, carry):
        at = pl.multiple_of(i * 80, 16)
        rows = qtab[pl.ds(at, 80), :].astype(F32) * base
        source = jnp.dot(rows.astype(BF16), ones, preferred_element_type=F32).astype(jnp.int32)
        lanes80 = lax.broadcasted_iota(jnp.int32, (80, 128), 1)
        for j in range(ROWS // LANES):
            hit = source == lanes80 + j * LANES
            oh[pl.ds(at, 80), pl.ds(j * LANES, LANES)] = jnp.where(hit, 1.0, 0.0).astype(BF16)
        return carry

    loads[2].wait()
    lax.fori_loop(0, 30, lay, 0)

    def build_windows(field, win):
        def one(oc, carry):
            for half in range(2):
                rows = oh[pl.ds(pl.multiple_of(oc * 800 + half * 400, 16), 400), :]
                padded = jnp.dot(rows, field[...], preferred_element_type=F32).reshape(5, 80, C)
                for ob in range(3):
                    part = padded[:, ob * 8 : ob * 8 + 64].reshape(320, C).astype(BF16)
                    lanes = pl.ds(pl.multiple_of((ob * 3 + oc) * C, C), C)
                    win[pl.ds(half * 320, 320), lanes] = part
            return carry

        lax.fori_loop(0, 3, one, 0)

    def conv(win, weight):
        for m in range(2):
            acc = jnp.zeros((256, C), F32)
            for oa in range(3):
                acc = acc + jnp.dot(
                    win[pl.ds(oa * 64 + m * 256, 256), :],
                    weight[pl.ds(oa * 9 * C, 9 * C), :],
                    preferred_element_type=F32,
                )
            yield m, acc

    def slope(value):
        sig = jax.nn.sigmoid(value)
        return sig * (1.0 + value * (1.0 - sig))

    def half_occ(m):
        part = occb[pl.ds(m * 256, 256), :]
        return jnp.concatenate([part, part], axis=1)

    def transpose_windows(win, turned):
        def one(j, carry):
            at = pl.ds(pl.multiple_of(j * C, C), C)
            turned[at, :] = win[:, at].T
            return carry

        lax.fori_loop(0, 9, one, 0)

    gpad[pl.ds(0, 64), :] = jnp.zeros((64, C), BF16)
    gpad[pl.ds(576, 64), :] = jnp.zeros((64, C), BF16)

    for copy in sent:
        copy.wait_recv()
    build_windows(um, win_m)
    loads[3].wait()
    for m, acc in conv(win_m, w1):
        value = acc * half_occ(m)
        pre[pl.ds(m * 256, 256), :] = value
        uh[pl.ds(m * 256, 256), :] = (value * jax.nn.sigmoid(value)).astype(BF16)
    sent = send_halo(1, uh)
    transpose_windows(win_m, tm)
    for copy in sent:
        copy.wait_recv()
    build_windows(uh, win_h)
    loads[4].wait()
    loads[5].wait()
    for m, acc in conv(win_h, w2):
        rows = pl.ds(m * 256, 256)
        value = acc * half_occ(m) + um[rows, :].astype(F32)
        grad = (cot[rows, :].astype(F32) * slope(value) * half_occ(m)).astype(BF16)
        ug[rows, :] = grad
        gpad[pl.ds(64 + m * 256, 256), :] = grad
    sent = send_halo(2, ug)
    transpose_windows(win_h, th)

    def weight_grad(unit, turned):
        k7 = unit % 7
        for ky in range(4):
            k = ky * 7 + k7
            if k < 27:
                rows = pl.ds((k % 9) * C, C)
                if k // 9 == 1:
                    left, right = turned[rows, :], gpad[...]
                else:
                    left, right = turned[rows, pl.ds((k // 9) * 64, VOX)], gpad[pl.ds(64, VOX), :]
                res = jnp.dot(left, right, preferred_element_type=F32).reshape(NZ, NX, 8, C)
            else:
                res = jnp.zeros((NZ, NX, 8, C), F32)
            for xx in range(NX):
                grads[0, xx, :, pl.ds(unit_row(unit, ky), 8), :] = res[:, xx, :, :LANES]
                grads[1, ky, :, pl.ds(unit_row(unit, xx), 8), :] = res[:, xx, :, LANES:]

    def unit_row(unit, b):
        lo, n = next(f for f in FLOWS if f[0] <= unit < f[0] + f[1])
        return lo * 32 + b * n * 8 + (unit - lo) * 8

    def pair_start(f):
        lo, n = FLOWS[f]
        part = pl.ds(lo * 32, n * 32)
        copies = []
        for j in range(4):
            block = near_b[(j + 1) % 4]

            def cast(i, carry):
                psend[block, i, part, :] = grads[not_core, block, i, part, :].astype(BF16)
                return carry

            lax.fori_loop(0, NZ, cast, 0, unroll=UNROLL)
            copies.append(
                push(
                    psend.at[block, :, part],
                    precv.at[block, :, part],
                    ps.at[f, j],
                    pr.at[f, j],
                    (d + not_core - core, s),
                )
            )
        return copies

    def ring_start(f, pairs):
        lo, n = FLOWS[f]
        part = pl.ds(lo * 32, n * 32)
        copies = []
        for j in range(4):
            block = near_a[(j + 1) % 4]
            pairs[j].wait_recv()

            def add(i, carry):
                total = grads[core, block, i, part, :] + precv[block, i, part, :].astype(F32)
                if j < 3:
                    asend[j, i, part, :] = total.astype(BF16)
                else:
                    grads[core, pa, i, part, :] = total
                return carry

            lax.fori_loop(0, NZ, add, 0, unroll=UNROLL)
            if j < 3:
                copies.append(
                    push(asend.at[j, :, part], arecv.at[j, :, part], as_.at[f, j], ar.at[f, j], ring_dev[j + 1])
                )
        return copies

    def plane_copy(f, j):
        lo, n = FLOWS[f]
        rows = pl.ds(pl.multiple_of(lo * 32 + near_b[j % 4] * (n * 8), 16), n * 8)
        return pltpu.make_async_remote_copy(
            src_ref=zsend.at[near_z[j // 4], rows],
            dst_ref=zrecv.at[j, pl.ds(lo * 8, n * 8)],
            send_sem=zs.at[f],
            recv_sem=zr.at[f],
            device_id=plane_dev(j),
            device_id_type=MESH,
        )

    def plane_all(f, sem):
        lo, n = FLOWS[f]
        here = zrecv.at[pl.ds(1, 31), pl.ds(lo * 8, n * 8)]
        return pltpu.make_async_copy(here, here, sem.at[f])

    def plane_start(f, before):
        lo, n = FLOWS[f]
        part = pl.ds(lo * 32, n * 32)
        for copy in before:
            copy.wait_recv()

        def add(i, carry):
            far = arecv[0, i, part, :].astype(F32) + arecv[1, i, part, :].astype(F32)
            total = grads[core, pa, i, part, :] + (far + arecv[2, i, part, :].astype(F32))
            grads[core, pa, i, part, :] = total
            zsend[i, part, :] = total.astype(BF16)
            return carry

        lax.fori_loop(0, NZ, add, 0, unroll=UNROLL)

        for j in range(1, 32):
            plane_copy(f, j).start()

    def gather_start(f):
        lo, n = FLOWS[f]
        part = pl.ds(lo * 8, n * 8)
        mine = pl.ds(pl.multiple_of(lo * 32 + pb * (n * 8), 8), n * 8)

        plane_all(f, zr).wait()
        total = grads[core, pa, z, mine, :]
        for j in range(1, 32):
            total = total + zrecv[j, part, :].astype(F32)
        gath[y, core, part, :] = total
        here = gath.at[y, core, part]
        return [
            push(here, here, gs.at[f, n_], gr.at[f, n_], group_dev(dy, dc))
            for n_, (dy, dc) in enumerate(relations)
        ]

    flow = [None] * len(FLOWS)

    def pair(f):
        flow[f] = pair_start(f)

    def ring(f):
        flow[f] = ring_start(f, flow[f])

    def plane(f):
        plane_start(f, flow[f])
        flow[f] = []

    def gather(f):
        flow[f] = gather_start(f)

    def units(f, which):
        lo, n = FLOWS[f]
        for unit in range(lo, lo + n):
            if unit // 7 == which:
                weight_grad(unit, (th, tm)[which])

    units(0, 0)
    pair(0)
    units(1, 0)
    ring(0)

    for copy in sent:
        copy.wait_recv()
    build_windows(ug, win_h)

    for m in range(2):
        acc = jnp.zeros((256, C), F32)
        for oa in range(3):
            weights = jnp.concatenate([w2[pl.ds((26 - oa * 9 - j) * C, C), :] for j in range(9)], axis=1)
            acc = acc + lax.dot_general(
                win_h[pl.ds(oa * 64 + m * 256, 256), :],
                weights,
                (((1,), (1,)), ((), ())),
                preferred_element_type=F32,
            )
        rows = pl.ds(m * 256, 256)
        gpad[pl.ds(64 + m * 256, 256), :] = (acc * slope(pre[rows, :]) * half_occ(m)).astype(BF16)
    units(1, 1)
    pair(1)
    units(2, 1)
    pair(2)
    ring(1)
    plane(0)
    units(3, 1)
    pair(3)
    ring(2)
    plane(1)
    ring(3)
    gather(0)
    plane(2)
    plane(3)
    gather(1)
    gather(2)
    gather(3)
    for copies in flow:
        for copy in copies:
            copy.wait_recv()
    out[...] = gath[...]
    for copy in pending:
        copy.wait_send()
    for f in range(len(FLOWS)):
        plane_all(f, zs).wait()


def local(features, occupancy, nbr_slots, send_mask, cotangent, weight_one, weight_two):
    vmem = pl.BlockSpec(memory_space=pltpu.VMEM)
    smem = pl.BlockSpec(memory_space=pltpu.SMEM)
    hbm = pl.BlockSpec(memory_space=pl.ANY)
    dma = pltpu.SemaphoreType.DMA
    res = pl.pallas_call(
        kernel,
        out_shape=jax.ShapeDtypeStruct((NY, 2, UNITS * 8, LANES), F32),
        in_specs=[hbm, vmem, vmem, smem, hbm, hbm, hbm, hbm, hbm],
        out_specs=vmem,
        scratch_shapes=[
            pltpu.VMEM((VOX, C), BF16),
            pltpu.VMEM((VOX, C), BF16),
            pltpu.VMEM((2400, 128), BF16),
            pltpu.VMEM((PAY, 256), F32),
            pltpu.VMEM((27 * C, C), BF16),
            pltpu.VMEM((27 * C, C), BF16),
            pltpu.VMEM((1, 128), jnp.int32),
            pltpu.VMEM((VOX, LANES), F32),
            pltpu.VMEM((6 * PAY, VOX), BF16),
            pltpu.VMEM((2400, ROWS), BF16),
            pltpu.VMEM((ROWS, C), BF16),
            pltpu.VMEM((ROWS, C), BF16),
            pltpu.VMEM((ROWS, C), BF16),
            pltpu.VMEM((3, 6 * PAY, C), BF16),
            pltpu.VMEM((640, 9 * C), BF16),
            pltpu.VMEM((640, 9 * C), BF16),
            pltpu.VMEM((9 * C, 640), BF16),
            pltpu.VMEM((9 * C, 640), BF16),
            pltpu.VMEM((640, C), BF16),
            pltpu.VMEM((VOX, C), F32),
            pltpu.VMEM((2, 4, NZ, ROWS_ALL, LANES), F32),
            pltpu.VMEM((4, NZ, ROWS_ALL, LANES), BF16),
            pltpu.VMEM((4, NZ, ROWS_ALL, LANES), BF16),
            pltpu.VMEM((3, NZ, ROWS_ALL, LANES), BF16),
            pltpu.VMEM((3, NZ, ROWS_ALL, LANES), BF16),
            pltpu.VMEM((NZ, ROWS_ALL, LANES), BF16),
            pltpu.VMEM((32, UNITS * 8, LANES), BF16),
            pltpu.VMEM((NY, 2, UNITS * 8, LANES), F32),
            dma((6,)),
            dma((3, 6)),
            dma((3, 6)),
            dma((len(FLOWS), 4)),
            dma((len(FLOWS), 4)),
            dma((len(FLOWS), 3)),
            dma((len(FLOWS), 3)),
            dma((len(FLOWS),)),
            dma((len(FLOWS),)),
            dma((len(FLOWS), 7)),
            dma((len(FLOWS), 7)),
        ],
        compiler_params=pltpu.CompilerParams(
            collective_id=0, has_side_effects=True, vmem_limit_bytes=60 * 1024 * 1024
        ),
    )(
        features.reshape(VOX, C),
        occupancy.reshape(1, VOX),
        nbr_slots.reshape(1, 26),
        send_mask.reshape(1, 6),
        cotangent.reshape(VOX, C),
        weight_one.reshape(27 * C, C),
        weight_two.reshape(27 * C, C),
        jnp.asarray(padded_table(), BF16),
        jnp.asarray(payload_table(), F32),
    )
    res = res.reshape(NY, 2, 2, 7, 8, LANES).transpose(2, 4, 0, 3, 1, 5).reshape(2, 8, KP, C)[:, :, :27]
    return res[1], res[0]


def solution(mesh):
    in_specs = (
        P("dp", "space", None, None),
        P("dp", "space", None),
        P("dp", "space", None),
        P("dp", "space", None),
        P("dp", "space", None, None),
        P(),
        P(),
    )
    out_specs = (P("space", None, None), P("space", None, None))
    return jax.shard_map(local, mesh=mesh, in_specs=in_specs, out_specs=out_specs, check_vma=False)
```

time: 101 us -> 81.5 us (0.81)
  Pallas kernels: 98.1 us -> 78.9 us
    pallas_call x1, Pallas kernels: 98.1 us -> 78.9 us  [local(): pl.pallas_call(kernel, out_shape=jax.ShapeDtypeStruct((NY, 2, UNITS * 8,...]
where the time goes in v2:
time: 81.5 us; the launch traced here: 81.4 us
  Pallas kernels  78.9 us (97%)
  local copies, waits for them, and re-layouts  1.84 us (2%)
    pallas_call x1, Pallas kernels, local(): pl.pallas_call(kernel, out_shape=jax.ShapeDtypeStruct((NY, 2, UNITS * 8,...  78.9 us

profile of v2, /device:TPU:1, one launch (start us, length us, event | category | flops | bytes accessed | tf_op | source)
XLA Modules:
  0.0 81.4 jit_solution(9157937576960527041)
XLA Ops:
  0.6 78.9 %shard_map.104 = f32[4,2,112,128]{3,2,1,0:T(8,128)} custom-call(bf16[512,256]{1,0:T(8,128)(2,1)} %bitcast.19, s32[1,512]{1,0:T(1,128)} %bitcast.21, s32[1,26]{1,0:T(1,128)} %bitcast.22, s32[1,6]{1,0:T(1,128)} %bitcast.23, bf16[512,256]{1,0:T(8,128)(2,1)} %bitcast.20, bf16[6912,256]{1,0:T(8,128)(2,1)} %bitcast.15, bf16[6912,256]{1,0:T(8,128)(2,1)} %bitcast.16, ...), custom_call_target="tpu_custom_call" | custom-call | tf_op jit(solution)/shard_map/pallas_call | solution.py:466
  79.5 1.0 %copy.11 = f32[2,8,4,7,2,128]{5,1,4,3,2,0:T(8,128)S(1)} copy(f32[2,8,4,7,2,128]{5,1,3,0,4,2:T(8,128)} %bitcast.17) | data formatting | bytes 917504 | tf_op jit(solution)/shard_map/transpose | solution.py:526
  80.6 0.8 slice_bitcast_fusion

commit v3 on v2

--- a/solution.py
+++ b/solution.py
@@ -16,9 +16,10 @@
 OWN = VOX
 ROWS = VOX + 6 * PAY
 KP = 28
+SPLIT = 2
 UNITS = 14
 UNROLL = 4
-FLOWS = ((0, 6), (6, 4), (10, 2), (12, 2))
+FLOWS = ((0, 2), (2, 4), (6, 4), (10, 2), (12, 2))
 ROWS_ALL = UNITS * 4 * 8
 LANES = 128
 F32 = jnp.float32
@@ -52,6 +53,13 @@
                             row = row * 8 + t
                         line[26] = row
     return table.reshape(3 * 800, 128)
+
+
+def own_table():
+    table = padded_table()
+    own = ~(table[:, :26] != 0).any(axis=1)
+    source = np.where(own, 64 * table[:, 27] + table[:, 26], -1)
+    return (source[:, None] == np.arange(OWN)[None, :]).astype(np.float32)
 
 
 def payload_table():
@@ -79,11 +87,11 @@
 
 
 def kernel(
-    feat_hbm, occ, nbr, send, cot_hbm, w1_hbm, w2_hbm, qtab_hbm, ptab_hbm,
+    feat_hbm, occ, nbr, send, cot_hbm, w1_hbm, w2_hbm, qtab_hbm, ptab_hbm, otab_hbm,
     out,
-    feat, cot, qtab, ptab, w1, w2, nbrv, occb, sel, oh, um, uh, ug, hsend, win_m, win_h, tm, th, gpad, pre, grads,
-    psend, precv, asend, arecv, zsend, zrecv, gath,
-    wsem, hs, hr, ps, pr, as_, ar, zs, zr, gs, gr,
+    feat, cot, qtab, ptab, w1, w2, nbrv, occb, sel, oh, um, uh, ug, hsend, own, win_m, win_h, tm, th, gpad, pre, grads,
+    psend, precv, asend, arecv, zsend, zrecv, lrecv, bsend, brecv, gath,
+    wsem, hs, hr, ps, pr, as_, ar, zs, zr, gs, gr, osem, bs, br,
 ):
     d = lax.axis_index("dp")
     s = lax.axis_index("space")
@@ -116,7 +124,7 @@
 
     loads = []
     for n, (src, dst) in enumerate(
-        ((ptab_hbm, ptab), (feat_hbm, feat), (qtab_hbm, qtab), (w1_hbm, w1), (cot_hbm, cot), (w2_hbm, w2))
+        ((ptab_hbm, ptab), (feat_hbm, feat), (qtab_hbm, qtab), (otab_hbm, oh.at[:, pl.ds(0, OWN)]), (w1_hbm, w1), (cot_hbm, cot), (w2_hbm, w2))
     ):
         loads.append(pltpu.make_async_copy(src, dst, wsem.at[n]))
         loads[-1].start()
@@ -196,19 +204,31 @@
         rows = qtab[pl.ds(at, 80), :].astype(F32) * base
         source = jnp.dot(rows.astype(BF16), ones, preferred_element_type=F32).astype(jnp.int32)
         lanes80 = lax.broadcasted_iota(jnp.int32, (80, 128), 1)
-        for j in range(ROWS // LANES):
+        for j in range(OWN // LANES, ROWS // LANES):
             hit = source == lanes80 + j * LANES
             oh[pl.ds(at, 80), pl.ds(j * LANES, LANES)] = jnp.where(hit, 1.0, 0.0).astype(BF16)
         return carry
 
     loads[2].wait()
-    lax.fori_loop(0, 30, lay, 0)
+    lax.fori_loop(0, 30, lay, 0, unroll=2)
+    loads[3].wait()
+
+    def lay_own(field):
+        def one(i, carry):
+            at = pl.ds(pl.multiple_of(i * 400, 16), 400)
+            rows = oh[at, pl.ds(0, OWN)]
+            own[at, :] = jnp.dot(rows, field[pl.ds(0, OWN), :], preferred_element_type=F32).astype(BF16)
+            return carry
+
+        lax.fori_loop(0, 6, one, 0)
 
     def build_windows(field, win):
         def one(oc, carry):
             for half in range(2):
-                rows = oh[pl.ds(pl.multiple_of(oc * 800 + half * 400, 16), 400), :]
-                padded = jnp.dot(rows, field[...], preferred_element_type=F32).reshape(5, 80, C)
+                at = pl.ds(pl.multiple_of(oc * 800 + half * 400, 16), 400)
+                rows = oh[at, pl.ds(OWN, 6 * PAY)]
+                halo = jnp.dot(rows, field[pl.ds(OWN, 6 * PAY), :], preferred_element_type=F32)
+                padded = (halo + own[at, :].astype(F32)).reshape(5, 80, C)
                 for ob in range(3):
                     part = padded[:, ob * 8 : ob * 8 + 64].reshape(320, C).astype(BF16)
                     lanes = pl.ds(pl.multiple_of((ob * 3 + oc) * C, C), C)
@@ -247,21 +267,23 @@
     gpad[pl.ds(0, 64), :] = jnp.zeros((64, C), BF16)
     gpad[pl.ds(576, 64), :] = jnp.zeros((64, C), BF16)
 
+    lay_own(um)
     for copy in sent:
         copy.wait_recv()
     build_windows(um, win_m)
-    loads[3].wait()
+    loads[4].wait()
     for m, acc in conv(win_m, w1):
         value = acc * half_occ(m)
         pre[pl.ds(m * 256, 256), :] = value
         uh[pl.ds(m * 256, 256), :] = (value * jax.nn.sigmoid(value)).astype(BF16)
     sent = send_halo(1, uh)
+    lay_own(uh)
     transpose_windows(win_m, tm)
     for copy in sent:
         copy.wait_recv()
     build_windows(uh, win_h)
-    loads[4].wait()
     loads[5].wait()
+    loads[6].wait()
     for m, acc in conv(win_h, w2):
         rows = pl.ds(m * 256, 256)
         value = acc * half_occ(m) + um[rows, :].astype(F32)
@@ -355,6 +377,42 @@
         here = zrecv.at[pl.ds(1, 31), pl.ds(lo * 8, n * 8)]
         return pltpu.make_async_copy(here, here, sem.at[f])
 
+    def line_copy(f, j):
+        lo, n = FLOWS[f]
+        part = pl.ds(lo * 32, n * 32)
+        return pltpu.make_async_remote_copy(
+            src_ref=zsend.at[near_z[j], part],
+            dst_ref=lrecv.at[j, part],
+            send_sem=zs.at[f],
+            recv_sem=zr.at[f],
+            device_id=plane_dev(4 * j),
+            device_id_type=MESH,
+        )
+
+    def line_all(f, sem):
+        lo, n = FLOWS[f]
+        here = lrecv.at[pl.ds(1, 7), pl.ds(lo * 32, n * 32)]
+        return pltpu.make_async_copy(here, here, sem.at[f])
+
+    def across_start(f):
+        lo, n = FLOWS[f]
+        part = pl.ds(lo * 32, n * 32)
+        line_all(f, zr).wait()
+        total = grads[core, pa, z, part, :]
+        for j in range(1, 8):
+            total = total + lrecv[j, part, :].astype(F32)
+        bsend[part, :] = total
+        return [
+            push(
+                bsend.at[pl.ds(pl.multiple_of(lo * 32 + near_b[j] * (n * 8), 8), n * 8)],
+                brecv.at[j, pl.ds(lo * 8, n * 8)],
+                bs.at[f, j],
+                br.at[f, j],
+                plane_dev(j),
+            )
+            for j in range(1, 4)
+        ]
+
     def plane_start(f, before):
         lo, n = FLOWS[f]
         part = pl.ds(lo * 32, n * 32)
@@ -370,26 +428,42 @@
 
         lax.fori_loop(0, NZ, add, 0, unroll=UNROLL)
 
-        for j in range(1, 32):
-            plane_copy(f, j).start()
+        if f < SPLIT:
+            for j in (4, 3, 5, 2, 6, 1, 7):
+                line_copy(f, j).start()
+        else:
+            for j in range(1, 32):
+                plane_copy(f, j).start()
 
     def gather_start(f):
         lo, n = FLOWS[f]
         part = pl.ds(lo * 8, n * 8)
         mine = pl.ds(pl.multiple_of(lo * 32 + pb * (n * 8), 8), n * 8)
 
-        plane_all(f, zr).wait()
-        total = grads[core, pa, z, mine, :]
-        for j in range(1, 32):
-            total = total + zrecv[j, part, :].astype(F32)
-        gath[y, core, part, :] = total
-        here = gath.at[y, core, part]
+        if f < SPLIT:
+            for copy in flow[f]:
+                copy.wait_recv()
+            total = bsend[mine, :]
+            for j in range(1, 4):
+                total = total + brecv[j, part, :]
+        else:
+            plane_all(f, zr).wait()
+            total = grads[core, pa, z, mine, :]
+            for j in range(1, 32):
+                total = total + zrecv[j, part, :].astype(F32)
+        gath[part, :] = total
+        here = gath.at[part]
+        there = out.at[y, core, part]
+        kept = pltpu.make_async_copy(here, there, osem.at[f])
+        kept.start()
+        owned.append(kept)
         return [
-            push(here, here, gs.at[f, n_], gr.at[f, n_], group_dev(dy, dc))
+            push(here, there, gs.at[f, n_], gr.at[f, n_], group_dev(dy, dc))
             for n_, (dy, dc) in enumerate(relations)
         ]
 
     flow = [None] * len(FLOWS)
+    owned = []
 
     def pair(f):
         flow[f] = pair_start(f)
@@ -400,6 +474,9 @@
     def plane(f):
         plane_start(f, flow[f])
         flow[f] = []
+
+    def across(f):
+        flow[f] = across_start(f)
 
     def gather(f):
         flow[f] = gather_start(f)
@@ -414,11 +491,14 @@
     pair(0)
     units(1, 0)
     ring(0)
+    pair(1)
+    units(2, 0)
+    lay_own(ug)
 
     for copy in sent:
         copy.wait_recv()
     build_windows(ug, win_h)
-
+    ring(1)
     for m in range(2):
         acc = jnp.zeros((256, C), F32)
         for oa in range(3):
@@ -431,31 +511,36 @@
             )
         rows = pl.ds(m * 256, 256)
         gpad[pl.ds(64 + m * 256, 256), :] = (acc * slope(pre[rows, :]) * half_occ(m)).astype(BF16)
-    units(1, 1)
-    pair(1)
     units(2, 1)
     pair(2)
-    ring(1)
     plane(0)
     units(3, 1)
     pair(3)
     ring(2)
+    units(4, 1)
+    pair(4)
     plane(1)
     ring(3)
+    ring(4)
+    across(0)
+    plane(2)
+    across(1)
     gather(0)
-    plane(2)
     plane(3)
     gather(1)
+    plane(4)
     gather(2)
     gather(3)
+    gather(4)
     for copies in flow:
         for copy in copies:
             copy.wait_recv()
-    out[...] = gath[...]
+    for kept in owned:
+        kept.wait()
     for copy in pending:
         copy.wait_send()
     for f in range(len(FLOWS)):
-        plane_all(f, zs).wait()
+        (line_all if f < SPLIT else plane_all)(f, zs).wait()
 
 
 def local(features, occupancy, nbr_slots, send_mask, cotangent, weight_one, weight_two):
@@ -466,8 +551,8 @@
     res = pl.pallas_call(
         kernel,
         out_shape=jax.ShapeDtypeStruct((NY, 2, UNITS * 8, LANES), F32),
-        in_specs=[hbm, vmem, vmem, smem, hbm, hbm, hbm, hbm, hbm],
-        out_specs=vmem,
+        in_specs=[hbm, vmem, vmem, smem, hbm, hbm, hbm, hbm, hbm, hbm],
+        out_specs=hbm,
         scratch_shapes=[
             pltpu.VMEM((VOX, C), BF16),
             pltpu.VMEM((VOX, C), BF16),
@@ -483,6 +568,7 @@
             pltpu.VMEM((ROWS, C), BF16),
             pltpu.VMEM((ROWS, C), BF16),
             pltpu.VMEM((3, 6 * PAY, C), BF16),
+            pltpu.VMEM((2400, C), BF16),
             pltpu.VMEM((640, 9 * C), BF16),
             pltpu.VMEM((640, 9 * C), BF16),
             pltpu.VMEM((9 * C, 640), BF16),
@@ -496,8 +582,11 @@
             pltpu.VMEM((3, NZ, ROWS_ALL, LANES), BF16),
             pltpu.VMEM((NZ, ROWS_ALL, LANES), BF16),
             pltpu.VMEM((32, UNITS * 8, LANES), BF16),
-            pltpu.VMEM((NY, 2, UNITS * 8, LANES), F32),
-            dma((6,)),
+            pltpu.VMEM((8, ROWS_ALL, LANES), BF16),
+            pltpu.VMEM((ROWS_ALL, LANES), F32),
+            pltpu.VMEM((4, UNITS * 8, LANES), F32),
+            pltpu.VMEM((UNITS * 8, LANES), F32),
+            dma((7,)),
             dma((3, 6)),
             dma((3, 6)),
             dma((len(FLOWS), 4)),
@@ -508,6 +597,9 @@
             dma((len(FLOWS),)),
             dma((len(FLOWS), 7)),
             dma((len(FLOWS), 7)),
+            dma((len(FLOWS),)),
+            dma((len(FLOWS), 4)),
+            dma((len(FLOWS), 4)),
         ],
         compiler_params=pltpu.CompilerParams(
             collective_id=0, has_side_effects=True, vmem_limit_bytes=60 * 1024 * 1024
@@ -522,6 +614,7 @@
         weight_two.reshape(27 * C, C),
         jnp.asarray(padded_table(), BF16),
         jnp.asarray(payload_table(), F32),
+        jnp.asarray(own_table(), BF16),
     )
     res = res.reshape(NY, 2, 2, 7, 8, LANES).transpose(2, 4, 0, 3, 1, 5).reshape(2, 8, KP, C)[:, :, :27]
     return res[1], res[0]

time: 81.5 us -> 77 us (0.945)
  Pallas kernels: 78.9 us -> 74.4 us
    pallas_call x1, Pallas kernels: 78.9 us -> 74.4 us  [local(): pl.pallas_call(kernel, out_shape=jax.ShapeDtypeStruct((NY, 2, UNITS * 8,...]
where the time goes in v3:
time: 77 us; the launch traced here: 76.8 us
  Pallas kernels  74.4 us (97%)
  local copies, waits for them, and re-layouts  1.84 us (2%)
    pallas_call x1, Pallas kernels, local(): pl.pallas_call(kernel, out_shape=jax.ShapeDtypeStruct((NY, 2, UNITS * 8,...  74.4 us

profile of v3, /device:TPU:1, one launch (start us, length us, event | category | flops | bytes accessed | tf_op | source)
XLA Modules:
  0.0 76.8 jit_solution(5564674498029545603)
XLA Ops:
  0.6 74.4 %shard_map.113 = f32[4,2,112,128]{3,2,1,0:T(8,128)} custom-call(bf16[512,256]{1,0:T(8,128)(2,1)} %bitcast.19, s32[1,512]{1,0:T(1,128)} %bitcast.21, s32[1,26]{1,0:T(1,128)} %bitcast.22, s32[1,6]{1,0:T(1,128)} %bitcast.23, bf16[512,256]{1,0:T(8,128)(2,1)} %bitcast.20, bf16[6912,256]{1,0:T(8,128)(2,1)} %bitcast.15, bf16[6912,256]{1,0:T(8,128)(2,1)} %bitcast.16, ...), custom_call_target="tpu_custom_call" | custom-call | tf_op jit(solution)/shard_map/pallas_call | solution.py:551
  75.0 1.0 %copy.12 = f32[2,8,4,7,2,128]{5,1,4,3,2,0:T(8,128)S(1)} copy(f32[2,8,4,7,2,128]{5,1,3,0,4,2:T(8,128)} %bitcast.17) | data formatting | bytes 917504 | tf_op jit(solution)/shard_map/transpose | solution.py:619
  76.0 0.8 %slice_bitcast_fusion = (f32[8,27,256]{2,0,1:T(8,128)}, f32[8,27,256]{2,0,1:T(8,128)}) fusion(f32[2,8,28,256]{3,1,2,0:T(8,128)S(1)} %bitcast.18), kind=kLoop, calls=%fused_computation | loop fusion | bytes 884736 | tf_op jit(solution)/shard_map/squeeze | solution.py:620

commit v4 on v3

--- a/solution.py
+++ b/solution.py
@@ -220,7 +220,7 @@
             own[at, :] = jnp.dot(rows, field[pl.ds(0, OWN), :], preferred_element_type=F32).astype(BF16)
             return carry
 
-        lax.fori_loop(0, 6, one, 0)
+        lax.fori_loop(0, 6, one, 0, unroll=2)
 
     def build_windows(field, win):
         def one(oc, carry):
@@ -262,7 +262,7 @@
             turned[at, :] = win[:, at].T
             return carry
 
-        lax.fori_loop(0, 9, one, 0)
+        lax.fori_loop(0, 9, one, 0, unroll=3)
 
     gpad[pl.ds(0, 64), :] = jnp.zeros((64, C), BF16)
     gpad[pl.ds(576, 64), :] = jnp.zeros((64, C), BF16)

time: 77 us -> 76.3 us (level)
  no operation moved by 1% of the time
where the time goes in v4:
time: 76.3 us; the launch traced here: 76.2 us
  Pallas kernels  73.7 us (97%)
  local copies, waits for them, and re-layouts  1.84 us (2%)
    pallas_call x1, Pallas kernels, local(): pl.pallas_call(kernel, out_shape=jax.ShapeDtypeStruct((NY, 2, UNITS * 8,...  73.7 us

profile of v4, /device:TPU:1, one launch (start us, length us, event | category | flops | bytes accessed | tf_op | source)
XLA Modules:
  0.0 76.2 jit_solution(3874277525674630834)
XLA Ops:
  0.6 73.7 %shard_map.113 = f32[4,2,112,128]{3,2,1,0:T(8,128)} custom-call(bf16[512,256]{1,0:T(8,128)(2,1)} %bitcast.19, s32[1,512]{1,0:T(1,128)} %bitcast.21, s32[1,26]{1,0:T(1,128)} %bitcast.22, s32[1,6]{1,0:T(1,128)} %bitcast.23, bf16[512,256]{1,0:T(8,128)(2,1)} %bitcast.20, bf16[6912,256]{1,0:T(8,128)(2,1)} %bitcast.15, bf16[6912,256]{1,0:T(8,128)(2,1)} %bitcast.16, ...), custom_call_target="tpu_custom_call" | custom-call | tf_op jit(solution)/shard_map/pallas_call | solution.py:551
  74.3 1.0 %copy.12 = f32[2,8,4,7,2,128]{5,1,4,3,2,0:T(8,128)S(1)} copy(f32[2,8,4,7,2,128]{5,1,3,0,4,2:T(8,128)} %bitcast.17) | data formatting | bytes 917504 | tf_op jit(solution)/shard_map/transpose | solution.py:619
  75.4 0.8 %slice_bitcast_fusion = (f32[8,27,256]{2,0,1:T(8,128)}, f32[8,27,256]{2,0,1:T(8,128)}) fusion(f32[2,8,28,256]{3,1,2,0:T(8,128)S(1)} %bitcast.18), kind=kLoop, calls=%fused_computation | loop fusion | bytes 884736 | tf_op jit(solution)/shard_map/squeeze | solution.py:620
